TPU v7x, 32 devices: a whole 2x2x4 slice. The times are simulated.
32 devices in a mesh: section: 2 (over core), dp: 4 (over y, x), seq: 4 (over z).
Axes of the slice: x: 2, y: 2, z: 4, core: 2. Of those that a mesh axis runs over, the one named last changes fastest.
Arguments:
- tokens: bfloat16 [16, 1024, 512], P('dp', 'seq'), may hold values from -6 to 6
- cotangent: bfloat16 [16, 1024, 512], P('dp', 'seq'), may hold values from -6 to 6
- tap_masks: int32 [2, 9, 16, 1024], P('section', None, 'dp', 'seq'), may hold values from 0 to 1, as said below
- conv_weight: bfloat16 [2, 512, 9, 512], P('section'), may hold values from -0.09375 to 0.09375
- up_weight: bfloat16 [2, 512, 2048], P('section'), may hold values from -0.25 to 0.25
- up_bias: float32 [2, 2048], P('section'), may hold values from -1.5 to 1.5
- down_weight: bfloat16 [2, 2048, 512], P('section'), may hold values from -0.125 to 0.125
- norm_gains: float32 [2, 512, 2], P('section'), may hold values from 0.25 to 1.75
- shift_terms: float32 [2, 512, 4], P('section'), may hold values from -1.5 to 1.5
Outputs:
- activations: bfloat16 [2, 16, 1024, 512], P('section', 'dp', 'seq')
- in_grads: float32 [2, 16, 1024, 512], P('section', 'dp', 'seq')
- conv_grad: float32 [2, 512, 9, 512], P('section', ('dp', 'seq'))
- up_grad: float32 [2, 512, 2048], P('section', ('dp', 'seq'))
- up_bias_grad: float32 [2, 2048], P('section', ('dp', 'seq'))
- down_grad: float32 [2, 2048, 512], P('section', ('dp', 'seq'))
- gain_grad: float32 [2, 512, 2], P('section', ('dp', 'seq'))
- shift_grad: float32 [2, 512, 4], P('section', ('dp', 'seq'))
Inputs may be any that keep to these rules, and one draw needn't show every extreme that they name: tap_masks[s, k, r, p] is 1 exactly when position p + (k - 4) * d of row r lies inside the row and in the same contig (a run of positions) as p, with d = 2 for s = 0 and 32 for s = 1.
All inputs are finite; a program needn't handle non-finite values.
Results may differ from a plain program's by a relative error of at most 0.0095.
Values may be sent and summed in bfloat16 or wider, within the bound.
A program may use at most 192 MiB of HBM per device.

v0:
```python
import jax
import jax.numpy as jnp
from jax import lax
from jax.sharding import PartitionSpec as P

KERNEL_TAPS = 9
DILATION_TIGHT = 2
DILATION_WIDE = 32
MICRO = 4


def extended(block, sides, width):
    for axis, dim in sides:
        count = lax.axis_size(axis)
        forward = [(i, i + 1) for i in range(count - 1)]
        backward = [(target, source) for source, target in forward]
        low = lax.ppermute(
            lax.slice_in_dim(block, block.shape[dim] - width, None, axis=dim), axis, forward
        )
        high = lax.ppermute(lax.slice_in_dim(block, 0, width, axis=dim), axis, backward)
        block = jnp.concatenate([low, block, high], axis=dim)
    return block


def from_behind(value, axis, steps):
    count = lax.axis_size(axis)
    leading, last = (max(0, -steps), min(count, count - steps))
    return lax.ppermute(value, axis, [(source, source + steps) for source in range(leading, last)])


def layer_norm(values):
    centred = values - jnp.mean(values, axis=-1, keepdims=True)
    return centred * lax.rsqrt(jnp.mean(centred * centred, axis=-1, keepdims=True) + 1e-05)


def conv_branch(conv_out, gain_vec, shift_vec):
    return layer_norm(jax.nn.gelu(conv_out)) * gain_vec + shift_vec


def ffn_branch(ffn_out, gain_vec, shift_vec):
    return layer_norm(ffn_out) * gain_vec + shift_vec


def over_rows(values):
    return jnp.sum(values.astype(jnp.float32), axis=(0, 1))


def tap_stack_of(padded_tokens, length, dilation_spacing, direction):
    border_width = KERNEL_TAPS // 2 * DILATION_WIDE
    tap_list = [
        lax.dynamic_slice_in_dim(
            padded_tokens,
            border_width + direction * (tap_index - KERNEL_TAPS // 2) * dilation_spacing,
            length,
            1,
        )
        for tap_index in range(KERNEL_TAPS)
    ]
    return jnp.stack(tap_list, axis=2)


def block_forward(input_tokens, tap_mask, dilation_spacing, weights):
    (
        kernel_weight,
        up_matrix,
        up_projection_bias,
        down_matrix,
        norm_scale_vector,
        shifted_columns,
    ) = weights
    length = input_tokens.shape[1]
    padded_tokens = extended(input_tokens, (("seq", 1),), KERNEL_TAPS // 2 * DILATION_WIDE)
    tap_stack = tap_stack_of(padded_tokens, length, dilation_spacing, 1) * tap_mask
    conv_out = (
        jnp.einsum("rpki,iko->rpo", tap_stack, kernel_weight, preferred_element_type=jnp.float32)
        + shifted_columns[:, 0]
    )
    mixed_sum = input_tokens.astype(jnp.float32) + conv_branch(
        conv_out, norm_scale_vector[:, 0], shifted_columns[:, 1]
    )
    mixed_low = mixed_sum.astype(jnp.bfloat16)
    hidden = (
        jnp.einsum("rpd,df->rpf", mixed_low, up_matrix, preferred_element_type=jnp.float32)
        + up_projection_bias
    )
    upper_low = jax.nn.gelu(hidden).astype(jnp.bfloat16)
    ffn_out = (
        jnp.einsum("rpf,fd->rpd", upper_low, down_matrix, preferred_element_type=jnp.float32)
        + shifted_columns[:, 2]
    )
    result = mixed_sum + ffn_branch(ffn_out, norm_scale_vector[:, 1], shifted_columns[:, 3])
    return (result, (tap_stack, conv_out, mixed_low, hidden, upper_low, ffn_out))


def block_backward(grad_result, tap_mask, dilation_spacing, weights, saved_parts):
    (
        kernel_weight,
        up_matrix,
        up_projection_bias,
        down_matrix,
        norm_scale_vector,
        shifted_columns,
    ) = weights
    tap_stack, conv_out, mixed_low, hidden, upper_low, ffn_out = saved_parts
    length = grad_result.shape[1]
    _, ffn_back = jax.vjp(ffn_branch, ffn_out, norm_scale_vector[:, 1], shifted_columns[:, 3])
    grad_ffn, grad_gain_two, grad_shift_three = ffn_back(grad_result)
    grad_ffn_low = grad_ffn.astype(jnp.bfloat16)
    grad_down = jnp.einsum(
        "rpf,rpd->fd", upper_low, grad_ffn_low, preferred_element_type=jnp.float32
    )
    grad_upper = jnp.einsum(
        "rpd,fd->rpf", grad_ffn_low, down_matrix, preferred_element_type=jnp.float32
    )
    _, gelu_back = jax.vjp(jax.nn.gelu, hidden)
    grad_hidden_low = gelu_back(grad_upper)[0].astype(jnp.bfloat16)
    grad_up = jnp.einsum(
        "rpd,rpf->df", mixed_low, grad_hidden_low, preferred_element_type=jnp.float32
    )
    grad_mixed = grad_result + jnp.einsum(
        "rpf,df->rpd", grad_hidden_low, up_matrix, preferred_element_type=jnp.float32
    )
    _, conv_back = jax.vjp(conv_branch, conv_out, norm_scale_vector[:, 0], shifted_columns[:, 1])
    grad_conv, grad_gain_one, grad_shift_one = conv_back(grad_mixed)
    kernel_gradient_lower = grad_conv.astype(jnp.bfloat16)
    grad_conv_w = jnp.einsum(
        "rpki,rpo->iko", tap_stack, kernel_gradient_lower, preferred_element_type=jnp.float32
    )
    padded_tokens = extended(kernel_gradient_lower, (("seq", 1),), KERNEL_TAPS // 2 * DILATION_WIDE)
    back_stack = tap_stack_of(padded_tokens, length, dilation_spacing, -1) * tap_mask[:, :, ::-1, :]
    grad_inputs = grad_mixed + jnp.einsum(
        "rpko,iko->rpi", back_stack, kernel_weight, preferred_element_type=jnp.float32
    )
    grad_gains = jnp.stack([grad_gain_one, grad_gain_two], axis=1)
    grad_shifts = jnp.stack(
        [
            over_rows(kernel_gradient_lower),
            grad_shift_one,
            over_rows(grad_ffn_low),
            grad_shift_three,
        ],
        axis=1,
    )
    return (
        grad_inputs,
        (grad_conv_w, grad_up, over_rows(grad_hidden_low), grad_down, grad_gains, grad_shifts),
    )


def per_device(
    tokens,
    cotangent,
    tap_masks,
    conv_weight,
    up_weight,
    up_bias,
    down_weight,
    norm_gains,
    shift_terms,
):
    is_leading_section = lax.axis_index("section") == 0
    dilation_spacing = jnp.where(is_leading_section, DILATION_TIGHT, DILATION_WIDE).astype(
        jnp.int32
    )
    weights = (
        conv_weight[0],
        up_weight[0],
        up_bias[0],
        down_weight[0],
        norm_gains[0],
        shift_terms[0],
    )
    row_count, length, features = tokens.shape
    micro_rows = row_count // MICRO
    mask_rows = jnp.transpose(tap_masks[0], (1, 2, 0)).astype(jnp.bfloat16)[..., None]

    def rows_of(values, micro_index):
        return lax.slice_in_dim(
            values, micro_index * micro_rows, (micro_index + 1) * micro_rows, axis=0
        )

    received = jnp.zeros((micro_rows, length, features), jnp.bfloat16)
    stored, saved_list, produced = ([], [], [])
    for tick_index in range(MICRO + 1):
        early_index = min(tick_index, MICRO - 1)
        late_index = max(tick_index - 1, 0)
        input_tokens = jnp.where(is_leading_section, rows_of(tokens, early_index), received)
        tap_mask = jnp.where(
            is_leading_section, rows_of(mask_rows, early_index), rows_of(mask_rows, late_index)
        )
        result, saved_parts = block_forward(input_tokens, tap_mask, dilation_spacing, weights)
        result_low = result.astype(jnp.bfloat16)
        stored.append((input_tokens, tap_mask))
        produced.append(result_low)
        if tick_index < MICRO:
            received = from_behind(result_low, "section", 1)
    activations = jnp.where(
        is_leading_section,
        jnp.concatenate(produced[:MICRO], axis=0),
        jnp.concatenate(produced[1:], axis=0),
    )
    returned = jnp.zeros((micro_rows, length, features), jnp.bfloat16)
    totals = None
    full_grads, low_grads = ([], [])
    for tick_index in range(MICRO + 1):
        slot_index = MICRO - tick_index
        input_tokens, tap_mask = stored[slot_index]
        saved_parts = block_forward(input_tokens, tap_mask, dilation_spacing, weights)[1]
        own_rows = rows_of(cotangent, max(MICRO - 1 - tick_index, 0)).astype(jnp.float32)
        if tick_index == MICRO:
            own_rows = jnp.zeros_like(own_rows)
        grad_result = jnp.where(is_leading_section, returned.astype(jnp.float32), own_rows)
        grad_inputs, grad_terms = block_backward(
            grad_result, tap_mask, dilation_spacing, weights, saved_parts
        )
        totals = grad_terms if totals is None else jax.tree.map(jnp.add, totals, grad_terms)
        grad_low = grad_inputs.astype(jnp.bfloat16)
        full_grads.append(grad_inputs)
        low_grads.append(grad_low.astype(jnp.float32))
        if tick_index < MICRO:
            returned = from_behind(grad_low, "section", -1)
    conv_total, up_total, up_bias_total, down_total, gain_total, shift_total = totals
    conv_total, up_total, up_bias_total, down_total, gain_total, shift_total = (
        lax.psum_scatter(conv_total, ("dp", "seq"), scatter_dimension=0, tiled=True),
        lax.psum_scatter(up_total, ("dp", "seq"), scatter_dimension=0, tiled=True),
        lax.psum_scatter(up_bias_total, ("dp", "seq"), scatter_dimension=0, tiled=True),
        lax.psum_scatter(down_total, ("dp", "seq"), scatter_dimension=0, tiled=True),
        lax.psum_scatter(gain_total, ("dp", "seq"), scatter_dimension=0, tiled=True),
        lax.psum_scatter(shift_total, ("dp", "seq"), scatter_dimension=0, tiled=True),
    )
    micro_grads = [
        jnp.where(
            is_leading_section, full_grads[MICRO - micro_index], low_grads[MICRO - 1 - micro_index]
        )
        for micro_index in range(MICRO)
    ]
    in_grads = jnp.concatenate(micro_grads, axis=0)
    return (
        activations[None],
        in_grads[None],
        conv_total[None],
        up_total[None],
        up_bias_total[None],
        down_total[None],
        gain_total[None],
        shift_total[None],
    )


def solution(mesh):
    placed = (
        P("dp", "seq", None),
        P("dp", "seq", None),
        P("section", None, "dp", "seq"),
        P("section", None, None, None),
        P("section", None, None),
        P("section", None),
        P("section", None, None),
        P("section", None, None),
        P("section", None, None),
    )
    return jax.shard_map(
        per_device,
        mesh=mesh,
        in_specs=placed,
        out_specs=(
            P("section", "dp", "seq", None),
            P("section", "dp", "seq", None),
            P("section", ("dp", "seq"), None, None),
            P("section", ("dp", "seq"), None),
            P("section", ("dp", "seq")),
            P("section", ("dp", "seq"), None),
            P("section", ("dp", "seq"), None),
            P("section", ("dp", "seq"), None),
        ),
        check_vma=False,
    )
```

profile of v0, /device:TPU:0, one launch (start us, length us, event | category | flops | bytes accessed | tf_op | source)
XLA Modules:
  0.0 931.7 jit_solution(735294866019868730)
XLA Ops:
  9.2 5.6 collective-permute-start
  19.2 2.8 collective-permute-done.1
  33.7 2.9 collective-permute-start.3
  39.8 4.1 collective-permute-done.4
  52.1 3.5 collective-permute-start.6
  58.8 4.1 collective-permute-done.7
  72.4 4.6 collective-permute-start.9
  88.1 4.4 collective-permute-start.12
  95.8 4.1 collective-permute-done.13
  115.0 3.1 collective-permute-start.14
  120.6 4.4 collective-permute-done.15
  127.2 3.9 fusion.264
  148.4 4.5 collective-permute-done.18
  155.2 4.7 fusion.454
  176.6 5.2 fusion.95
  183.1 3.4 fusion.453
  187.9 5.2 fusion.98
  200.1 3.9 collective-permute-start.23
  205.5 5.1 fusion.101
  216.5 5.2 fusion.104
  233.8 18.8 %add_bitcast_fusion = f32[512,9,512]{0,2,1:T(8,128)} fusion(f32[512,9,512]{2,0,1:T(8,128)} %fusion.104, f32[512,9,512]{2,0,1:T(8,128)} %fusion.101, f32[512,9,512]{2,0,1:T(8,128)} %fusion.95, f32[512,9,512]{2,0,1:T(8,128)} %fusion.98, bf16[256,9,512]{2,0,1:T(8,128)(2,1)} %copy-done.45, bf16[256,9]{0,1:T(8,128)(2,1)S(1)} %copy-done.104, ...), kind=kOutput, calls=%fused_computation | convolution fusion | flops 1222115328 | bytes 49811968 | tf_op jit(solution)/shard_map/rpki,rpo->iko/dot_general | solution.py:126
  252.7 16.7 %copy.36 = f32[512,9,512]{2,1,0:T(8,128)} copy(f32[512,9,512]{0,2,1:T(8,128)} %add_bitcast_fusion) | data formatting | bytes 18874368 | tf_op jit(solution)/shard_map/add | solution.py:216
  269.4 2.7 fusion.388
  276.9 3.7 add_add_fusion
  287.9 3.5 add_add_fusion.1
  295.8 3.1 collective-permute-start.26
  300.2 41.0 %all-reduce = f32[2048]{0:T(1024)S(1)} all-reduce(f32[2048]{0:T(1024)S(1)} %add_add_fusion.12), channel_id=4, replica_groups=mesh['section'=2,'dp'=4,'seq'=4] {'dp','seq'}, use_global_device_ids=true, to_apply=%region_47.48.clone | all-reduce | flops 2048 | bytes 16384
  343.1 37.4 %reduce-scatter.18.cloned.1.call-done = f32[32,4]{1,0:T(8,128)} async-done(((f32[512,4]{1,0:T(8,128)}), f32[32,4]{1,0:T(8,128)}) %reduce-scatter.18.cloned.1.call-update) | async-done | bytes 528
  383.1 4.3 fusion.284
  388.9 340.3 %reduce-scatter.10.cloned.1.call-done = f32[32,9,512]{2,1,0:T(8,128)} async-done(((f32[512,9,512]{2,1,0:T(8,128)}), f32[32,9,512]{2,1,0:T(8,128)}) %reduce-scatter.10.cloned.1.call-update) | async-done | bytes 589840 | tf_op jit(solution)/shard_map/reduce_scatter | solution.py:224
  731.6 95.7 %reduce-scatter.14.cloned.1.call-done = f32[128,512]{1,0:T(8,128)} async-done(((f32[2048,512]{1,0:T(8,128)}), f32[128,512]{1,0:T(8,128)}) %reduce-scatter.14.cloned.1.call-update) | async-done | bytes 262160 | tf_op jit(solution)/shard_map/reduce_scatter | solution.py:227
  827.3 97.4 %reduce-scatter.12.cloned.1.call-done = f32[32,2048]{1,0:T(8,128)} async-done(((f32[512,2048]{1,0:T(8,128)}), f32[32,2048]{1,0:T(8,128)}) %reduce-scatter.12.cloned.1.call-update) | async-done | bytes 262160 | tf_op jit(solution)/shard_map/reduce_scatter | solution.py:225
  (669 shorter events, 164.5 us)
Async XLA Ops:
  7.2 334.6 %reduce-scatter.16.cloned.1.call-start = ((), (), s32[]{:S(2)}) async-start(), calls=%async_computation.8 | async-start | bytes 278528
  9.2 10.0 %collective-permute-start = (bf16[1,128,512]{2,1,0:T(8,128)(2,1)}, bf16[1,128,512]{2,1,0:T(8,128)(2,1)}, u32[]{:S(2)}, u32[]{:S(2)}) collective-permute-start(bf16[1,128,512]{2,1,0:T(8,128)(2,1)} %get-tuple-element.127), channel_id=1, source_target_pairs={{0,1},{1,2},{2,3},{4,5},{5,6},{6,7},{8,9},{9,10},{10,11},{12,13},{... | collective-permute-start | bytes 393224 | tf_op jit(solution)/shard_map/ppermute | solution.py:17
  14.8 7.2 collective-permute-start.1
  31.2 2.4 collective-permute-start.2
  33.7 6.1 collective-permute-start.3
  36.6 7.4 collective-permute-start.4
  49.6 2.4 collective-permute-start.5
  52.1 6.7 collective-permute-start.6
  55.6 7.4 collective-permute-start.7
  71.1 7.7 collective-permute-start.10
  72.4 7.6 collective-permute-start.9
  85.6 2.4 collective-permute-start.11
  88.1 7.7 collective-permute-start.12
  92.5 7.4 collective-permute-start.13
  115.0 5.6 collective-permute-start.14
  118.0 7.0 collective-permute-start.15
  131.1 3.6 collective-permute-start.16
  143.4 5.1 collective-permute-start.17
  145.7 7.2 collective-permute-start.18
  159.9 3.8 collective-permute-start.19
  173.1 8.7 collective-permute-start.20
  175.0 7.4 collective-permute-start.21
  186.5 6.6 collective-permute-start.22
  200.1 10.6 %collective-permute-start.23 = (bf16[1,128,512]{2,1,0:T(8,128)(2,1)S(1)}, bf16[1,128,512]{2,1,0:T(8,128)(2,1)S(1)}, u32[]{:S(2)}, u32[]{:S(2)}) collective-permute-start(bf16[1,128,512]{2,1,0:T(8,128)(2,1)S(1)} %get-tuple-element.111), channel_id=1, source_target_pairs={{0,1},{1,2},{2,3},{4,5},{5,6},{6,7},{8,9},{9,10},{10,11},{12,13},{... | collective-permute-start | bytes 393224 | tf_op jit(solution)/shard_map/ppermute | solution.py:17
  204.0 8.1 collective-permute-start.24
  215.1 6.6 collective-permute-start.25
  229.5 151.0 %reduce-scatter.18.cloned.1.call-start = ((), (), s32[]{:S(2)}) async-start(), calls=%async_computation.9 | async-start | bytes 278528
  233.5 495.7 %reduce-scatter.10.cloned.1.call-start = ((), (), s32[]{:S(2)}) async-start(), calls=%async_computation.5 | async-start | bytes 17825792 | tf_op jit(solution)/shard_map/reduce_scatter | solution.py:224
  269.4 558.0 %reduce-scatter.14.cloned.1.call-start = ((), (), s32[]{:S(2)}) async-start(), calls=%async_computation.7 | async-start | bytes 4456448 | tf_op jit(solution)/shard_map/reduce_scatter | solution.py:227
  280.7 644.0 %reduce-scatter.12.cloned.1.call-start = ((), (), s32[]{:S(2)}) async-start(), calls=%async_computation.6 | async-start | bytes 4456448 | tf_op jit(solution)/shard_map/reduce_scatter | solution.py:225
  295.8 86.1 %collective-permute-start.26 = (bf16[1,128,512]{2,1,0:T(8,128)(2,1)S(1)}, bf16[1,128,512]{2,1,0:T(8,128)(2,1)S(1)}, u32[]{:S(2)}, u32[]{:S(2)}) collective-permute-start(bf16[1,128,512]{2,1,0:T(8,128)(2,1)S(1)} %get-tuple-element.109), channel_id=1, source_target_pairs={{0,1},{1,2},{2,3},{4,5},{5,6},{6,7},{8,9},{9,10},{10,11},{12,13},{... | collective-permute-start | bytes 393224 | tf_op jit(solution)/shard_map/ppermute | solution.py:17
  298.9 83.0 %collective-permute-start.27 = (bf16[1,128,512]{2,1,0:T(8,128)(2,1)S(1)}, bf16[1,128,512]{2,1,0:T(8,128)(2,1)S(1)}, u32[]{:S(2)}, u32[]{:S(2)}) collective-permute-start(bf16[1,128,512]{2,1,0:T(8,128)(2,1)S(1)} %get-tuple-element.110), channel_id=1, source_target_pairs={{1,0},{2,1},{3,2},{5,4},{6,5},{7,6},{9,8},{10,9},{11,10},{13,12},{... | collective-permute-start | bytes 393224 | tf_op jit(solution)/shard_map/ppermute | solution.py:20
  (184 other events, 1044.0 us)
Sparse Core Ops, SparseCore 0:
  229.6 75.8 reduce-scatter.15
  307.8 72.6 reduce-scatter.17
  382.8 346.3 reduce-scatter.9
  732.0 95.2 reduce-scatter.13
  830.0 94.6 reduce-scatter.11
where the time goes:
time: 941 us; the launch traced here: 932 us
  waiting for transfers between devices  614 us (65%)
  matrix products  113 us (12%)
  starting transfers between devices  60.9 us (6%)
  local copies, waits for them, and re-layouts  52.5 us (6%)
  blocking collectives  41 us (4%)
  other arithmetic  32.3 us (3%)
  between operations  18.1 us (2%)
    reduce_scatter x1, waiting for transfers between devices, per_device(): lax.psum_scatter(conv_total, ('dp', 'seq'), scatter_dimension=0, tiled=True)  340 us
    reduce_scatter x1, waiting for transfers between devices, per_device(): lax.psum_scatter(up_total, ('dp', 'seq'), scatter_dimension=0, tiled=True)  97.4 us
    reduce_scatter x1, waiting for transfers between devices, per_device(): lax.psum_scatter(down_total, ('dp', 'seq'), scatter_dimension=0, tiled=True)  95.7 us
    unnamed x1, blocking collectives  41 us
    dot_general x5, matrix products, block_backward(): jnp.einsum('rpki,rpo->iko', tap_stack, kernel_gradient_lower, preferred_e...  39.5 us
    unnamed x7, waiting for transfers between devices  37.5 us
    ppermute x10, starting transfers between devices, extended(): lax.ppermute(lax.slice_in_dim(block, block.shape[dim] - width, None, axis...  35.2 us
    unnamed x451, local copies, waits for them, and re-layouts  28.2 us
  transfers between devices with their start and end apart: 33, of which 24 were waited for; matrix products, arithmetic and copies ran while one was open for 11% of the time, Pallas kernels for 0%

commit v1 on v0

v1 whole, which is shorter than its diff:
```python
import functools

import jax
import jax.numpy as jnp
from jax import lax
from jax.experimental import pallas as pl
from jax.experimental.pallas import tpu as pltpu
from jax.sharding import PartitionSpec as P

TAPS = 9
CENTRE = TAPS // 2
TIGHT = 2
WIDE = 32
HALO = CENTRE * WIDE
EDGE = 16
EPS = 1e-05
MESH = pl.DeviceIdType.MESH
BF16 = jnp.bfloat16
F32 = jnp.float32
LAGS = (0, 3, 5, 7)
TANH_SCALE = 0.7978845608028654
TANH_CUBE = TANH_SCALE * 0.044715


def gelu_pair(z):
    square = z * z
    half = 0.5 + 0.5 * jnp.tanh(z * (TANH_SCALE + TANH_CUBE * square))
    value = z * half
    return value, half + value * (1.0 - half) * (2.0 * TANH_SCALE + 6.0 * TANH_CUBE * square)


def normalise(values):
    centred = values - jnp.mean(values, axis=-1, keepdims=True)
    scale = lax.rsqrt(jnp.mean(centred * centred, axis=-1, keepdims=True) + EPS)
    return centred * scale, scale


def norm_backward(weighted, unit):
    return (
        weighted
        - jnp.mean(weighted, axis=-1, keepdims=True)
        - unit * jnp.mean(weighted * unit, axis=-1, keepdims=True)
    )


def column_sum(values):
    return jnp.sum(values, axis=0, keepdims=True)


def dot(a, b):
    return jnp.dot(a, b, preferred_element_type=F32)


def dot_nt(a, b):
    return lax.dot_general(a, b, (((1,), (1,)), ((), ())), preferred_element_type=F32)


def dot_tn(a, b):
    return lax.dot_general(a, b, (((0,), (0,)), ((), ())), preferred_element_type=F32)


class Geometry:
    def __init__(self, dp, seq, rows, length, width, hidden):
        self.dp, self.seq = dp, seq
        self.rows, self.length, self.width = rows, length, width
        self.tokens = rows * length
        self.chunks = hidden // width
        self.low = max(1, 16 * dp * seq // width)
        self.owners = dp * seq // self.low
        self.share = width // self.owners
        self.final_share = width // (dp * seq)
        self.bias_share = hidden // (dp * seq)
        dp_bits = [("dp", 1 << i) for i in range(dp.bit_length() - 1)]
        seq_all = [("seq", 1 << i) for i in range(seq.bit_length() - 1)]
        seq_bits = [bit for bit in seq_all if bit[1] >= self.low]
        self.bits = dp_bits + seq_bits
        self.all_bits = dp_bits + seq_all
        back = dp_bits[::-1]
        first = seq_bits[:1]
        orders = [
            dp_bits + seq_bits,
            back + seq_bits,
            first + dp_bits + seq_bits[1:],
            dp_bits + seq_bits,
            back + seq_bits,
            first + back + seq_bits[1:],
        ]
        self.orders = [[self.bits.index(bit) for bit in order] for order in orders]
        self.stages = len(self.bits)
        self.slices = 2 * self.chunks + TAPS
        lags = list(LAGS)
        while len(lags) < self.stages:
            lags.append(lags[-1] + 2)
        self.lags = lags[: self.stages]
        self.last_lag = self.lags[-1] + 1


def body(
    geo,
    tokens_hbm,
    cotangent_hbm,
    conv_hbm,
    up_hbm,
    down_hbm,
    masks,
    bias,
    gains,
    shifts,
    act_hbm,
    grads_hbm,
    conv_out,
    up_out,
    down_out,
    bias_out,
    gain_out,
    shift_out,
    fields,
    conv_grads,
    conv_w,
    up_w,
    down_w,
    slabs,
    taps,
    unit_one,
    slope_one,
    unit_two,
    scale_two,
    mixed_grads,
    given,
    ffn_grads,
    results,
    mask_columns,
    partial,
    arrived,
    sums,
    sums_sent,
    sums_arrived,
    load_sem,
    row_load_sem,
    token_edge_send,
    token_edge_recv,
    pass_send,
    pass_recv,
    back_send,
    back_recv,
    edge_send,
    edge_recv,
    act_sem,
    grads_sem,
    part_send,
    part_recv,
    sums_send,
    sums_recv,
):
    rows, length, width, chunks = geo.rows, geo.length, geo.width, geo.chunks
    section = lax.axis_index("section")
    dp = lax.axis_index("dp")
    seq = lax.axis_index("seq")
    mine = {"dp": dp, "seq": seq}
    in_first = section == 0
    in_second = section == 1
    has_left = (seq + geo.seq - 1) // geo.seq
    has_right = 1 - (seq + 1) // geo.seq
    own = slice(HALO, HALO + length)

    def bit_of(bit):
        axis, size = bit
        return (mine[axis] // size) % 2

    def partner(bit):
        axis, size = bit
        other = mine[axis] + (1 - 2 * bit_of(bit)) * size
        return (section, other, seq) if axis == "dp" else (section, dp, other)

    core = (1 - section, dp, seq)
    left, right = (section, dp, seq - 1), (section, dp, seq + 1)

    loads = [
        pltpu.make_async_copy(conv_hbm, conv_w, load_sem.at[0]),
        pltpu.make_async_copy(up_hbm, up_w, load_sem.at[1]),
        pltpu.make_async_copy(down_hbm, down_w, load_sem.at[2]),
    ]
    token_load = pltpu.make_async_copy(tokens_hbm, fields.at[:, own], row_load_sem.at[0])
    given_load = pltpu.make_async_copy(cotangent_hbm, given, row_load_sem.at[1])

    @pl.when(in_first)
    def _():
        token_load.start()

    for load in loads:
        load.start()

    @pl.when(in_second)
    def _():
        given_load.start()

    @pl.when(has_left == 0)
    def _():
        fields[:, :HALO] = jnp.zeros((rows, HALO, width), BF16)
        conv_grads[:, :HALO] = jnp.zeros((rows, HALO, width), BF16)

    @pl.when(has_right == 0)
    def _():
        fields[:, HALO + length :] = jnp.zeros((rows, HALO, width), BF16)
        conv_grads[:, HALO + length :] = jnp.zeros((rows, HALO, width), BF16)

    sums[...] = jnp.zeros(sums.shape, F32)

    barrier = pltpu.get_barrier_semaphore()
    for bit in geo.all_bits:
        pl.semaphore_signal(barrier, inc=1, device_id=partner(bit), device_id_type=MESH)
    pl.semaphore_signal(barrier, inc=1, device_id=core, device_id_type=MESH)

    @pl.when(has_left == 1)
    def _():
        for who in (section, 1 - section):
            pl.semaphore_signal(barrier, inc=1, device_id=(who, dp, seq - 1), device_id_type=MESH)

    @pl.when(has_right == 1)
    def _():
        for who in (section, 1 - section):
            pl.semaphore_signal(barrier, inc=1, device_id=(who, dp, seq + 1), device_id_type=MESH)

    pl.semaphore_wait(barrier, len(geo.all_bits) + 1 + 2 * has_left + 2 * has_right)

    tokens_right = pltpu.make_async_remote_copy(
        src_ref=tokens_hbm.at[:, length - EDGE : length],
        dst_ref=fields.at[:, HALO - EDGE : HALO],
        send_sem=token_edge_send.at[0],
        recv_sem=token_edge_recv.at[0],
        device_id=right,
        device_id_type=MESH,
    )
    tokens_left = pltpu.make_async_remote_copy(
        src_ref=tokens_hbm.at[:, 0:EDGE],
        dst_ref=fields.at[:, HALO + length : HALO + length + EDGE],
        send_sem=token_edge_send.at[1],
        recv_sem=token_edge_recv.at[1],
        device_id=left,
        device_id_type=MESH,
    )

    @pl.when(in_first)
    def _():
        pl.when(has_right == 1)(tokens_right.start)
        pl.when(has_left == 1)(tokens_left.start)

    for r in range(rows):
        plane = masks[:, r, :].astype(F32)
        padded = jnp.concatenate([plane, jnp.zeros((128 - TAPS, length), F32)], axis=0)
        mask_columns[r * length : (r + 1) * length, :] = jnp.transpose(padded)

    def span(m):
        return pl.ds(pl.multiple_of(m * length, length), length)

    def tap_list(source, m, dilation):
        mask_rows = mask_columns[span(m), :]
        for k in range(TAPS):
            values = source[m, pl.ds(HALO + (k - CENTRE) * dilation, length), :]
            if k != CENTRE:
                lane = jnp.broadcast_to(mask_rows[:, k : k + 1], (length, 128)).astype(BF16)
                values = values * jnp.concatenate([lane] * (width // 128), axis=1)
            yield k, values

    def pass_copies(m):
        return (
            pltpu.make_async_remote_copy(
                src_ref=results.at[m],
                dst_ref=fields.at[m, own],
                send_sem=pass_send.at[m, 0],
                recv_sem=pass_recv.at[m, 0],
                device_id=(1, dp, seq),
                device_id_type=MESH,
            ),
            pltpu.make_async_remote_copy(
                src_ref=results.at[m, length - HALO : length],
                dst_ref=fields.at[m, 0:HALO],
                send_sem=pass_send.at[m, 1],
                recv_sem=pass_recv.at[m, 1],
                device_id=(1, dp, seq + 1),
                device_id_type=MESH,
            ),
            pltpu.make_async_remote_copy(
                src_ref=results.at[m, 0:HALO],
                dst_ref=fields.at[m, HALO + length : HALO + length + HALO],
                send_sem=pass_send.at[m, 2],
                recv_sem=pass_recv.at[m, 2],
                device_id=(1, dp, seq - 1),
                device_id_type=MESH,
            ),
        )

    def back_copy(m):
        return pltpu.make_async_remote_copy(
            src_ref=results.at[m],
            dst_ref=given.at[m],
            send_sem=back_send.at[m],
            recv_sem=back_recv.at[m],
            device_id=(0, dp, seq),
            device_id_type=MESH,
        )

    def edge_copies(m, reach):
        return (
            pltpu.make_async_remote_copy(
                src_ref=conv_grads.at[m, HALO + length - reach : HALO + length],
                dst_ref=conv_grads.at[m, HALO - reach : HALO],
                send_sem=edge_send.at[m, 0],
                recv_sem=edge_recv.at[m, 0],
                device_id=right,
                device_id_type=MESH,
            ),
            pltpu.make_async_remote_copy(
                src_ref=conv_grads.at[m, HALO : HALO + reach],
                dst_ref=conv_grads.at[m, HALO + length : HALO + length + reach],
                send_sem=edge_send.at[m, 1],
                recv_sem=edge_recv.at[m, 1],
                device_id=left,
                device_id_type=MESH,
            ),
        )

    def act_copy(m):
        return pltpu.make_async_copy(results.at[m], act_hbm.at[m], act_sem.at[m])

    def grads_copy(m):
        return pltpu.make_async_copy(mixed_grads.at[m], grads_hbm.at[m], grads_sem.at[m])

    loads[0].wait()
    loads[1].wait()
    loads[2].wait()

    @pl.when(in_first)
    def _():
        token_load.wait()
        pl.when(has_left == 1)(tokens_right.wait_recv)
        pl.when(has_right == 1)(tokens_left.wait_recv)

    gain_one, gain_two = gains[0:1, :], gains[1:2, :]
    shift_conv, shift_one = shifts[0:1, :], shifts[1:2, :]
    shift_ffn, shift_two = shifts[2:3, :], shifts[3:4, :]

    def forward(m, carry):
        here = span(m)

        @pl.when(in_second)
        def _():
            whole, low, high = pass_copies(m)
            whole.wait_recv()
            pl.when(has_left == 1)(low.wait_recv)
            pl.when(has_right == 1)(high.wait_recv)

        for flag, dilation in ((in_first, TIGHT), (in_second, WIDE)):

            @pl.when(flag)
            def _(dilation=dilation):
                for k, values in tap_list(fields, m, dilation):
                    taps[:, k * width : (k + 1) * width] = values

        value, slope = gelu_pair(dot(taps[...], conv_w[...]) + shift_conv)
        unit, scale = normalise(value)
        unit_one[here, :] = unit.astype(BF16)
        slope_one[here, :] = (slope * scale).astype(BF16)
        mixed = fields[m, own, :].astype(F32) + unit * gain_one + shift_one
        mixed_low = mixed.astype(BF16)
        slabs[2 * chunks, here, :] = mixed_low
        ffn = None
        for c in range(chunks):
            part = slice(c * width, (c + 1) * width)
            value, slope = gelu_pair(dot(mixed_low, up_w[:, part]) + bias[:, part])
            low = value.astype(BF16)
            slabs[c, here, :] = low
            slabs[chunks + c, here, :] = slope.astype(BF16)
            term = dot(low, down_w[part, :])
            ffn = term if ffn is None else ffn + term
        unit, scale = normalise(ffn + shift_ffn)
        unit_two[here, :] = unit.astype(BF16)
        scale_two[here, :] = jnp.broadcast_to(scale, (length, 128))
        results[m] = (mixed + unit * gain_two + shift_two).astype(BF16)
        act_copy(m).start()

        @pl.when(in_first)
        def _():
            whole, low, high = pass_copies(m)
            pl.when(has_right == 1)(low.start)
            pl.when(has_left == 1)(high.start)
            whole.start()

        return carry

    lax.fori_loop(0, rows, forward, 0)

    @pl.when(in_second)
    def _():
        given_load.wait()

    def backward_ffn(m, carry):
        here = span(m)

        @pl.when(in_first)
        def _():
            back_copy(m).wait_recv()

        grad = given[m].astype(F32)
        unit = unit_two[here, :].astype(F32)
        grad_ffn = norm_backward(grad * gain_two, unit) * scale_two[here, 0:1]
        sums[1:2, :] += column_sum(grad * unit)
        sums[5:6, :] += column_sum(grad)
        sums[4:5, :] += column_sum(grad_ffn)
        grad_ffn_low = grad_ffn.astype(BF16)
        ffn_grads[here, :] = grad_ffn_low
        mixed = grad
        for c in range(chunks):
            part = slice(c * width, (c + 1) * width)
            grad_hidden = dot_nt(grad_ffn_low, down_w[part, :]) * slabs[chunks + c, here, :].astype(F32)
            sums[8 + c : 9 + c, :] += column_sum(grad_hidden)
            low = grad_hidden.astype(BF16)
            slabs[chunks + c, here, :] = low
            mixed = mixed + dot_nt(low, up_w[:, part])
        mixed_grads[m] = mixed
        unit = unit_one[here, :].astype(F32)
        grad_conv = norm_backward(mixed * gain_one, unit) * slope_one[here, :].astype(F32)
        sums[0:1, :] += column_sum(mixed * unit)
        sums[3:4, :] += column_sum(mixed)
        sums[2:3, :] += column_sum(grad_conv)
        conv_grads[m, own, :] = grad_conv.astype(BF16)
        for flag, reach in ((in_first, EDGE), (in_second, HALO)):

            @pl.when(flag)
            def _(reach=reach):
                low, high = edge_copies(m, reach)
                pl.when(has_right == 1)(low.start)
                pl.when(has_left == 1)(high.start)

        return carry

    lax.fori_loop(0, rows, backward_ffn, 0)

    def sums_copy(i):
        return pltpu.make_async_remote_copy(
            src_ref=sums_sent.at[i],
            dst_ref=sums_arrived.at[i],
            send_sem=sums_send.at[i],
            recv_sem=sums_recv.at[i],
            device_id=partner(geo.all_bits[i]),
            device_id_type=MESH,
        )

    def sums_begin(i):
        sums_sent[i] = sums[...]
        sums_copy(i).start()

    def sums_end(i):
        sums_copy(i).wait_recv()
        sums[...] += sums_arrived[i]

    my_bits = [bit_of(bit) for bit in geo.bits]
    owners, share = geo.owners, geo.share

    def is_order(j, t):
        off = j % 6 - t
        return 1 - (off * off + 35) // 36

    def bit_weights(j):
        picked = [is_order(j, t) for t in range(6)]
        return [
            sum(picked[t] * (owners >> (1 + geo.orders[t].index(b))) for t in range(6))
            for b in range(geo.stages)
        ]

    def place(weights, owner_dp, owner_seq):
        where = 0
        for b, (axis, size) in enumerate(geo.bits):
            index = owner_dp if axis == "dp" else owner_seq * geo.low
            where = where + ((index // size) % 2 + my_bits[b]) % 2 * weights[b]
        return where

    def part_copy(j, i):
        half = owners >> (i + 1)
        picked = [is_order(j, t) for t in range(6)]
        to = {"dp": dp, "seq": seq}
        for b, (axis, size) in enumerate(geo.bits):
            chosen = sum(picked[t] for t in range(6) if geo.orders[t][i] == b)
            to[axis] = to[axis] + chosen * (1 - 2 * my_bits[b]) * size
        return pltpu.make_async_remote_copy(
            src_ref=partial.at[j, half : 2 * half],
            dst_ref=arrived.at[j, half : 2 * half],
            send_sem=part_send.at[j, i],
            recv_sem=part_recv.at[j, i],
            device_id=(section, to["dp"], to["seq"]),
            device_id_type=MESH,
        )

    def take(j, i):
        half = owners >> (i + 1)
        part_copy(j, i).wait_recv()
        return partial[j, 0:half].astype(F32) + arrived[j, half : 2 * half].astype(F32)

    def advance(j, i):
        half = owners >> i
        partial[j, 0:half] = take(j, i - 1).astype(BF16)
        part_copy(j, i).start()

    def finish(j):
        total = take(j, geo.stages - 1)[0]

        @pl.when(j < chunks)
        def _():
            up_out[:, pl.ds(pl.multiple_of(j * width, width), width)] = total

        @pl.when((j >= chunks) & (j < 2 * chunks))
        def _():
            down_out[pl.ds(pl.multiple_of((j - chunks) * share, share), share), :] = total

        @pl.when(j >= 2 * chunks)
        def _():
            conv_out[j - 2 * chunks] = total

    down_turn = 2 * chunks - 1
    conv_turn = 2 * chunks + rows
    end_turn = conv_turn + TAPS

    def at_turn(turn, act):
        pl.when((turn >= 0) & (turn < chunks))(lambda: act(turn))
        pl.when((turn >= down_turn) & (turn < down_turn + chunks))(lambda: act(turn - down_turn + chunks))
        pl.when((turn >= conv_turn) & (turn < end_turn))(lambda: act(turn - conv_turn + 2 * chunks))

    def events(turn):
        at_turn(turn - geo.last_lag, finish)
        for i in range(geo.stages - 1, 0, -1):
            at_turn(turn - geo.lags[i], lambda j, i=i: advance(j, i))

    def row_slice(j, grad):
        weights = bit_weights(j)
        for owner in range(owners):
            where = place(weights, owner // (geo.seq // geo.low), owner % (geo.seq // geo.low))
            partial[j, where] = grad[owner * share : (owner + 1) * share].astype(BF16)
        part_copy(j, 0).start()

    def up_slice(j, carry):
        row_slice(j, dot_tn(slabs[2 * chunks], slabs[chunks + j]))
        events(j)
        return carry

    def down_slab(c, carry):
        grad = dot_tn(slabs[c], ffn_grads[...])
        each = owners // chunks
        per_dp = geo.seq // geo.low
        for jj in range(chunks):
            weights = bit_weights(chunks + jj)
            for w in range(each):
                owner = c * each + w
                where = place(weights, owner // per_dp, owner % per_dp)
                at = (w * chunks + jj) * share
                partial[chunks + jj, where] = grad[at : at + share].astype(BF16)

        @pl.when(c == chunks - 1)
        def _():
            for jj in range(chunks):
                part_copy(chunks + jj, 0).start()

        events(chunks + c)
        return carry

    sums_begin(0)
    lax.fori_loop(0, chunks, up_slice, 0)
    sums_end(0)
    sums_begin(1)
    lax.fori_loop(0, chunks, down_slab, 0)
    sums_end(1)
    sums_begin(2)

    def settle_forward(m, carry):
        act_copy(m).wait()

        @pl.when(in_first)
        def _():
            whole, low, high = pass_copies(m)
            pl.when(has_right == 1)(low.wait_send)
            pl.when(has_left == 1)(high.wait_send)
            whole.wait_send()

        return carry

    lax.fori_loop(0, rows, settle_forward, 0)

    def backward_conv(m, carry):
        here = span(m)
        for flag, dilation, reach in ((in_first, TIGHT, EDGE), (in_second, WIDE, HALO)):

            @pl.when(flag)
            def _(dilation=dilation, reach=reach):
                low, high = edge_copies(m, reach)
                pl.when(has_left == 1)(low.wait_recv)
                pl.when(has_right == 1)(high.wait_recv)
                for k, values in tap_list(conv_grads, m, dilation):
                    slabs[TAPS - 1 - k, here, :] = values

        grad = mixed_grads[m]
        for k in range(TAPS):
            grad = grad + dot_nt(slabs[k, here, :], conv_w[k * width : (k + 1) * width, :])
        mixed_grads[m] = grad

        @pl.when(in_second)
        def _():
            low = grad.astype(BF16)
            results[m] = low
            back_copy(m).start()
            mixed_grads[m] = low.astype(F32)

        grads_copy(m).start()
        events(2 * chunks + m)
        return carry

    lax.fori_loop(0, rows, backward_conv, 0)
    sums_end(2)
    if len(geo.all_bits) > 3:
        sums_begin(3)

    def gather_fields(m, carry):
        ffn_grads[span(m), :] = fields[m, own, :]
        return carry

    lax.fori_loop(0, rows, gather_fields, 0)

    def conv_slice(k, carry):
        j = 2 * chunks + k
        row_slice(j, dot_tn(ffn_grads[...], slabs[k]))
        events(conv_turn + k)
        return carry

    lax.fori_loop(0, TAPS, conv_slice, 0)
    for i in range(3, len(geo.all_bits)):
        sums_end(i)
        if i + 1 < len(geo.all_bits):
            sums_begin(i + 1)

    index = dp * geo.seq + seq
    lane = lax.broadcasted_iota(jnp.int32, (128, width), 1)
    line = lax.broadcasted_iota(jnp.int32, (128, width), 0)
    exact = functools.partial(
        lax.dot_general,
        dimension_numbers=(((1,), (1,)), ((), ())),
        precision=lax.Precision.HIGHEST,
        preferred_element_type=F32,
    )
    picked = exact(sums[...], (lane == line + index * geo.final_share).astype(F32))
    gain_out[...] = picked[0:2, : geo.final_share]
    shift_out[...] = picked[2:6, : geo.final_share]
    start = index * geo.bias_share
    picked = exact(sums[...], (lane == line + start % width).astype(F32))
    wanted = lax.broadcasted_iota(jnp.int32, picked.shape, 0) == 8 + start // width
    bias_out[...] = column_sum(jnp.where(wanted, picked, 0.0))[:, : geo.bias_share]

    def drain(turn, carry):
        events(turn)
        return carry

    lax.fori_loop(end_turn, end_turn + geo.last_lag, drain, 0)

    def settle_slice(j, carry):
        for i in range(geo.stages):
            part_copy(j, i).wait_send()
        return carry

    lax.fori_loop(0, geo.slices, settle_slice, 0)
    for i in range(len(geo.all_bits)):
        sums_copy(i).wait_send()

    def settle_row(m, carry):
        grads_copy(m).wait()
        for flag, reach in ((in_first, EDGE), (in_second, HALO)):

            @pl.when(flag)
            def _(reach=reach):
                low, high = edge_copies(m, reach)
                pl.when(has_right == 1)(low.wait_send)
                pl.when(has_left == 1)(high.wait_send)

        pl.when(in_second)(back_copy(m).wait_send)
        return carry

    lax.fori_loop(0, rows, settle_row, 0)

    @pl.when(in_first)
    def _():
        pl.when(has_right == 1)(tokens_right.wait_send)
        pl.when(has_left == 1)(tokens_left.wait_send)


def per_device(
    dp,
    seq,
    tokens,
    cotangent,
    tap_masks,
    conv_weight,
    up_weight,
    up_bias,
    down_weight,
    norm_gains,
    shift_terms,
):
    rows, length, width = tokens.shape
    hidden = up_weight.shape[2]
    geo = Geometry(dp, seq, rows, length, width, hidden)
    reach = length + 2 * HALO
    vmem = pl.BlockSpec(memory_space=pltpu.VMEM)
    hbm = pl.BlockSpec(memory_space=pl.ANY)
    dma = pltpu.SemaphoreType.DMA
    stages = len(geo.all_bits)
    slices = (geo.slices, geo.owners, geo.share, width)
    act, grads, conv_grad, up_grad, down_grad, bias_grad, gain_grad, shift_grad = pl.pallas_call(
        functools.partial(body, geo),
        out_shape=[
            jax.ShapeDtypeStruct((rows, length, width), BF16),
            jax.ShapeDtypeStruct((rows, length, width), F32),
            jax.ShapeDtypeStruct((TAPS, geo.share, width), F32),
            jax.ShapeDtypeStruct((geo.share, hidden), F32),
            jax.ShapeDtypeStruct((geo.chunks * geo.share, width), F32),
            jax.ShapeDtypeStruct((1, geo.bias_share), F32),
            jax.ShapeDtypeStruct((2, geo.final_share), F32),
            jax.ShapeDtypeStruct((4, geo.final_share), F32),
        ],
        in_specs=[hbm] * 5 + [vmem] * 4,
        out_specs=[hbm] * 2 + [vmem] * 6,
        scratch_shapes=[
            pltpu.VMEM((rows, reach, width), BF16),
            pltpu.VMEM((rows, reach, width), BF16),
            pltpu.VMEM((TAPS * width, width), BF16),
            pltpu.VMEM((width, hidden), BF16),
            pltpu.VMEM((hidden, width), BF16),
            pltpu.VMEM((TAPS, geo.tokens, width), BF16),
            pltpu.VMEM((length, TAPS * width), BF16),
            pltpu.VMEM((geo.tokens, width), BF16),
            pltpu.VMEM((geo.tokens, width), BF16),
            pltpu.VMEM((geo.tokens, width), BF16),
            pltpu.VMEM((geo.tokens, 128), F32),
            pltpu.VMEM((rows, length, width), F32),
            pltpu.VMEM((rows, length, width), BF16),
            pltpu.VMEM((geo.tokens, width), BF16),
            pltpu.VMEM((rows, length, width), BF16),
            pltpu.VMEM((geo.tokens, 128), F32),
            pltpu.VMEM(slices, BF16),
            pltpu.VMEM(slices, BF16),
            pltpu.VMEM((16, width), F32),
            pltpu.VMEM((stages, 16, width), F32),
            pltpu.VMEM((stages, 16, width), F32),
            dma((3,)),
            dma((2,)),
            dma((2,)),
            dma((2,)),
            dma((rows, 3)),
            dma((rows, 3)),
            dma((rows,)),
            dma((rows,)),
            dma((rows, 2)),
            dma((rows, 2)),
            dma((rows,)),
            dma((rows,)),
            dma((geo.slices, geo.stages)),
            dma((geo.slices, geo.stages)),
            dma((stages,)),
            dma((stages,)),
        ],
        compiler_params=pltpu.CompilerParams(
            collective_id=0, has_side_effects=True, vmem_limit_bytes=63 * 2**20
        ),
    )(
        tokens,
        cotangent,
        jnp.transpose(conv_weight[0], (1, 0, 2)).reshape(TAPS * width, width),
        up_weight[0],
        down_weight[0],
        tap_masks[0],
        up_bias,
        jnp.transpose(norm_gains[0]),
        jnp.transpose(shift_terms[0]),
    )
    conv_grad = jnp.transpose(conv_grad, (1, 0, 2))
    if geo.low > 1:
        groups = [list(range(at, at + geo.low)) for at in range(0, seq, geo.low)]
        conv_grad, up_grad, down_grad = (
            lax.psum_scatter(
                grad, "seq", scatter_dimension=0, axis_index_groups=groups, tiled=True
            )
            for grad in (conv_grad, up_grad, down_grad)
        )
    return (
        act[None],
        grads[None],
        conv_grad[None],
        up_grad[None],
        bias_grad,
        down_grad[None],
        jnp.transpose(gain_grad)[None],
        jnp.transpose(shift_grad)[None],
    )


def solution(mesh):
    placed = (
        P("dp", "seq", None),
        P("dp", "seq", None),
        P("section", None, "dp", "seq"),
        P("section", None, None, None),
        P("section", None, None),
        P("section", None),
        P("section", None, None),
        P("section", None, None),
        P("section", None, None),
    )
    return jax.shard_map(
        functools.partial(per_device, mesh.shape["dp"], mesh.shape["seq"]),
        mesh=mesh,
        in_specs=placed,
        out_specs=(
            P("section", "dp", "seq", None),
            P("section", "dp", "seq", None),
            P("section", ("dp", "seq"), None, None),
            P("section", ("dp", "seq"), None),
            P("section", ("dp", "seq")),
            P("section", ("dp", "seq"), None),
            P("section", ("dp", "seq"), None),
            P("section", ("dp", "seq"), None),
        ),
        check_vma=False,
    )
```

time: 941 us -> 177 us (0.19)
  waiting for transfers between devices: 614 us -> 0 us
  Pallas kernels: 0 us -> 168 us
  matrix products: 113 us -> 0 us
  starting transfers between devices: 60.9 us -> 0 us
  local copies, waits for them, and re-layouts: 52.5 us -> 7.71 us
  blocking collectives: 41 us -> 0 us
  other arithmetic: 32.3 us -> 0 us
  between operations: 18.1 us -> 0.67 us
    reduce_scatter x3 -> x0, waiting for transfers between devices: 533 us -> none  [the longest x1 340 us: per_device(): lax.psum_scatter(conv_total, ('dp', 'seq'), scatter_dimension=0, tiled=True)]
    pallas_call x0 -> x1, Pallas kernels: none -> 168 us  [per_device(): pl.pallas_call(functools.partial(body, geo), out_shape=[jax.ShapeDtypeStr...]
    dot_general x45 -> x0, matrix products: 113 us -> none  [the longest x5 39.5 us: block_backward(): jnp.einsum('rpki,rpo->iko', tap_stack, kernel_gradient_lower, preferred_e...]
    ppermute x28 -> x0, starting transfers between devices: 60.1 us -> none  [the longest x10 35.2 us: extended(): lax.ppermute(lax.slice_in_dim(block, block.shape[dim] - width, None, axis...]
    ppermute x28 -> x0, waiting for transfers between devices: 43.2 us -> none  [the longest x10 28 us: extended(): lax.ppermute(lax.slice_in_dim(block, 0, width, axis=dim), axis, backward)]
    unnamed x1 -> x0, blocking collectives: 41 us -> none
    unnamed x7 -> x0, waiting for transfers between devices: 37.5 us -> none
    unnamed x451 -> x22, local copies, waits for them, and re-layouts: 28.2 us -> 7.71 us
  transfers between devices with their start and end apart: 33 -> 0, of which waited for: 24 -> 0; matrix products, arithmetic and copies ran while one was open for 11% -> 0% of each run, Pallas kernels for 0% -> 0%
where the time goes in v1:
time: 177 us; the launch traced here: 176 us
  Pallas kernels  168 us (95%)
  local copies, waits for them, and re-layouts  7.71 us (4%)
    pallas_call x1, Pallas kernels, per_device(): pl.pallas_call(functools.partial(body, geo), out_shape=[jax.ShapeDtypeStr...  168 us
    unnamed x22, local copies, waits for them, and re-layouts  7.71 us

profile of v1, /device:TPU:0, one launch (start us, length us, event | category | flops | bytes accessed | tf_op | source)
XLA Modules:
  0.0 176.4 jit_solution(7492245700770407616)
XLA Ops:
  0.6 168.0 %shard_map.152 = (bf16[4,256,512]{2,1,0:T(8,128)(2,1)}, f32[4,256,512]{2,1,0:T(8,128)}, f32[9,32,512]{2,1,0:T(8,128)}, f32[32,2048]{1,0:T(8,128)}, f32[128,512]{...) custom-call(bf16[4,256,512]{2,1,0:T(8,128)(2,1)} %tokens_hbm.1, ...), custom_call_target="tpu_custom_call" | custom-call | tf_op jit(solution)/shard_map/pallas_call | solution.py:713
  168.6 0.0 copy-start
  168.6 2.4 %copy.25 = bf16[1,4,256,512]{3,2,1,0:T(8,128)(2,1)} copy(bf16[1,4,256,512]{3,2,1,0:T(8,128)(2,1)} %bitcast.31) | data formatting | bytes 2097152
  171.1 0.0 copy-done
  171.1 0.0 copy-start.1
  171.1 0.0 copy-start.3
  171.1 0.0 copy-start.6
  171.1 0.0 copy-start.2
  171.1 1.3 copy.26
  172.4 0.1 copy-done.1
  172.5 0.0 copy-start.5
  172.5 0.0 copy-start.4
  172.5 0.8 copy.27
  173.3 0.0 copy-done.3
  173.3 0.7 copy.28
  174.0 0.0 copy-done.6
  174.0 0.5 copy.29
  174.5 0.0 copy-done.2
  174.5 0.7 copy.30
  175.2 0.0 copy-done.5
  175.2 0.6 copy.31
  175.8 0.0 copy-done.4
  175.8 0.6 copy.32
Async XLA Ops:
  168.6 2.4 %copy-start = (f32[4,256,512]{2,1,0:T(8,128)S(1)}, f32[4,256,512]{2,1,0:T(8,128)}, u32[]{:S(2)}) copy-start(f32[4,256,512]{2,1,0:T(8,128)} %get-tuple-element.17) | copy-start | bytes 6291460
  171.1 1.4 copy-start.1
  171.1 2.2 %copy-start.3 = (f32[32,2048]{1,0:T(8,128)S(1)}, f32[32,2048]{1,0:T(8,128)}, u32[]{:S(2)}) copy-start(f32[32,2048]{1,0:T(8,128)} %get-tuple-element.19) | copy-start | bytes 786436
  171.1 2.9 %copy-start.6 = (f32[1,128]{1,0:T(1,128)S(1)}, f32[1,128]{1,0:T(1,128)}, u32[]{:S(2)}) copy-start(f32[1,128]{1,0:T(1,128)} %get-tuple-element.36) | copy-start | bytes 1540
  171.1 3.5 %copy-start.2 = (f32[128,512]{1,0:T(8,128)S(1)}, f32[128,512]{1,0:T(8,128)}, u32[]{:S(2)}) copy-start(f32[128,512]{1,0:T(8,128)} %get-tuple-element.21) | copy-start | bytes 786436
  172.5 2.7 %copy-start.5 = (f32[2,32]{1,0:T(2,128)S(1)}, f32[2,32]{1,0:T(2,128)}, u32[]{:S(2)}) copy-start(f32[2,32]{1,0:T(2,128)} %get-tuple-element.22) | copy-start | bytes 772
  172.5 3.3 %copy-start.4 = (f32[4,32]{1,0:T(4,128)S(1)}, f32[4,32]{1,0:T(4,128)}, u32[]{:S(2)}) copy-start(f32[4,32]{1,0:T(4,128)} %get-tuple-element.23) | copy-start | bytes 1540
